TPU v7x, 32 devices: a whole 2x2x4 slice. The times are simulated.
32 devices in a mesh: groups: 2 (over x), tensor: 8 (over z, y), seq: 2 (over core).
Axes of the slice: x: 2, y: 2, z: 4, core: 2. Of those that a mesh axis runs over, the one named last changes fastest.
Arguments:
- tokens: bfloat16 [4, 256, 3584], P(('groups', 'seq'), 'tensor'), parts along dimension 0, may hold values from -2048 to 2048
- section_of_row: int32 [1024], P('groups'), parts along dimension 0, may hold values from 0 to 7, never falling along the last dimension, each value on 1 to 128 neighbouring positions
- section_kind: int32 [16], P('groups'), parts along dimension 0, may hold values 0 or 1
- norm_gain: bfloat16 [2, 3584], replicated, may hold values from 0.099609375 to 1.8984375
- qkv_weight: bfloat16 [2, 3584, 4608], P(None, None, 'tensor'), may hold values from -4 to 4
- qkv_bias: bfloat16 [2, 4608], P(None, 'tensor'), may hold values from -3 to 3
- out_weight: bfloat16 [2, 3584, 3584], P(None, 'tensor'), may hold values from -0.09375 to 0.09375
Outputs:
- attn_out: bfloat16 [4, 256, 3584], P(('groups', 'seq'), 'tensor'), parts along dimension 0
There are 2 independent parts, one for each index of `groups`. A program takes and returns all parts, laid end to end along the dimension named above; an argument that names none is the same for every part. Nothing has to cross between parts.
Inputs may be any that keep to these rules, and one draw needn't show every extreme that they name: `section_of_row`: section numbers never fall along the rows; each section holds 1 to 128 rows and one holds exactly 128. `section_kind`: 1 marks an image section, 0 a text section.
All inputs are finite; a program needn't handle non-finite values.
Results may differ from a plain program's by a relative error of at most 0.024.
Values may be sent and summed in bfloat16 or wider, within the bound.
A program may use at most 64 MiB of HBM per device.

v0:
```python
import math

import jax
import jax.numpy as jnp
from jax import lax
from jax.sharding import PartitionSpec as P

QUERY_HEADS = 28
KEY_VALUE_HEADS = 4
HEAD_SIZE = 128


NORM_EPSILON = 1e-06
ROPE_THETA = 1000000.0
BLOCKED_SCORE = -1e30


def row_kinds(section_of_row, section_kind):
    labels = jnp.arange(section_kind.shape[0], dtype=jnp.int32)
    matches = section_of_row[:, None] == labels[None, :]
    return jnp.sum(jnp.where(matches, section_kind[None, :], 0), axis=1)


def apply_rotation(value_matrix, token_places, head_count):
    row_count = value_matrix.shape[0]
    head_dim = value_matrix.shape[1] // head_count
    field_rows = value_matrix.astype(jnp.float32).reshape(row_count, head_count, head_dim)
    frequencies = ROPE_THETA ** (-(jnp.arange(0, head_dim, 2, dtype=jnp.float32) / head_dim))
    angles = token_places.astype(jnp.float32)[:, None] * frequencies[None, :]
    angles = jnp.concatenate([angles, angles], axis=1)
    cosine = jnp.cos(angles)[:, None, :]
    sine_part = jnp.sin(angles)[:, None, :]
    first_half = field_rows[:, :, : head_dim // 2]
    second_half = field_rows[:, :, head_dim // 2 :]
    turned = jnp.concatenate([-second_half, first_half], axis=2)
    rotated = field_rows * cosine + turned * sine_part
    return rotated.reshape(row_count, head_count * head_dim).astype(jnp.bfloat16)


def both_kinds(row_slab, weights, kind_rows):
    first_kind = jnp.dot(row_slab, weights[0], preferred_element_type=jnp.float32)
    second_kind = jnp.dot(row_slab, weights[1], preferred_element_type=jnp.float32)
    return jnp.where(kind_rows[:, None] == 1, second_kind, first_kind)


def project_rows(row_slab, weights, kind_rows):
    return both_kinds(row_slab, weights, kind_rows)


def body(tokens, section_of_row, section_kind, norm_gain, qkv_weight, qkv_bias, out_weight):
    tensor_size = lax.axis_size("tensor")
    tensor_rank = lax.axis_index("tensor")
    seq_rank = lax.axis_index("seq")
    own_rows = tokens.shape[1]
    group_rows = own_rows * tensor_size
    query_span_width = QUERY_HEADS * HEAD_SIZE
    key_value_width = KEY_VALUE_HEADS * HEAD_SIZE
    queries_per_group = QUERY_HEADS // KEY_VALUE_HEADS
    kinds_all = row_kinds(section_of_row, section_kind)
    group_start = seq_rank * group_rows
    kinds_group = lax.dynamic_slice_in_dim(kinds_all, group_start, group_rows)
    own_kinds = lax.dynamic_slice_in_dim(kinds_group, tensor_rank * own_rows, own_rows)
    features = tokens[0].astype(jnp.float32)
    gain_rows = jnp.where(own_kinds[:, None] == 1, norm_gain[1], norm_gain[0]).astype(jnp.float32)
    scaled = lax.rsqrt(jnp.mean(features * features, axis=1, keepdims=True) + NORM_EPSILON)
    normed = (features * scaled * gain_rows).astype(jnp.bfloat16)
    bias_pair = qkv_bias.astype(jnp.float32)
    product = project_rows(
        lax.all_gather(normed, "tensor", axis=0, tiled=True), qkv_weight, kinds_group
    )
    column_block = (
        product + jnp.where(kinds_group[:, None] == 1, bias_pair[1], bias_pair[0])
    ).astype(jnp.bfloat16)
    iota_own = jnp.arange(own_rows, dtype=jnp.int32)
    key_places = group_start + tensor_rank * own_rows + iota_own
    row_tile = lax.all_to_all(column_block, "tensor", split_axis=0, concat_axis=1, tiled=True)
    query_matrix = apply_rotation(row_tile[:, :query_span_width], key_places, QUERY_HEADS)
    key_row_values = apply_rotation(
        row_tile[:, query_span_width : query_span_width + key_value_width],
        key_places,
        KEY_VALUE_HEADS,
    )
    value_matrix = row_tile[:, query_span_width + key_value_width :]
    query_sections = jnp.take(section_of_row, key_places)
    query_image = jnp.take(kinds_all, key_places) == 1
    section_last = (
        jnp.sum((section_of_row[None, :] <= query_sections[:, None]).astype(jnp.int32), axis=1) - 1
    )
    reach_rows = jnp.where(query_image, section_last, key_places)
    reach_most = jnp.max(reach_rows)
    query_total = query_matrix.shape[0]
    grouped_queries = (
        query_matrix.reshape(query_total, KEY_VALUE_HEADS, queries_per_group, HEAD_SIZE)
        .transpose(1, 0, 2, 3)
        .reshape(KEY_VALUE_HEADS, query_total * queries_per_group, HEAD_SIZE)
    )
    scale_factor = 1.0 / math.sqrt(HEAD_SIZE)

    def attend_block(state_in, key_block):
        key_tile, value_tile, key_pos = key_block
        window_keys = key_pos.shape[0]
        key_sections = jnp.take(section_of_row, key_pos)
        allowed = (key_pos[None, :] <= key_places[:, None]) | (
            key_sections[None, :] == query_sections[:, None]
        ) & query_image[:, None]
        allowed = jnp.broadcast_to(
            allowed[:, None, :], (query_total, queries_per_group, window_keys)
        ).reshape(1, query_total * queries_per_group, window_keys)
        key_head_tensor = key_tile.reshape(window_keys, KEY_VALUE_HEADS, HEAD_SIZE)
        value_head_tensor = value_tile.reshape(window_keys, KEY_VALUE_HEADS, HEAD_SIZE)

        def update(state_now):
            running_max, running_sum, running_acc = state_now
            scores = (
                jnp.einsum(
                    "gqa,kga->gqk",
                    grouped_queries,
                    key_head_tensor,
                    preferred_element_type=jnp.float32,
                )
                * scale_factor
            )
            scores = jnp.where(allowed, scores, BLOCKED_SCORE)
            new_max = jnp.maximum(running_max, jnp.max(scores, axis=2))
            shrink = jnp.exp(running_max - new_max)
            weights = jnp.where(allowed, jnp.exp(scores - new_max[:, :, None]), 0.0)
            new_sum = running_sum * shrink + jnp.sum(weights, axis=2)
            new_acc = running_acc * shrink[:, :, None] + jnp.einsum(
                "gqk,kga->gqa",
                weights.astype(jnp.bfloat16),
                value_head_tensor,
                preferred_element_type=jnp.float32,
            )
            return (new_max, new_sum, new_acc)

        return (
            lax.cond(jnp.min(key_pos) > reach_most, lambda state_now: state_now, update, state_in),
            None,
        )

    initial = (
        jnp.full((KEY_VALUE_HEADS, query_total * queries_per_group), BLOCKED_SCORE, jnp.float32),
        jnp.zeros((KEY_VALUE_HEADS, query_total * queries_per_group), jnp.float32),
        jnp.zeros((KEY_VALUE_HEADS, query_total * queries_per_group, HEAD_SIZE), jnp.float32),
    )
    slab_keys = lax.all_gather(key_row_values, ("tensor", "seq"), axis=0, tiled=True)
    slab_values = lax.all_gather(value_matrix, ("tensor", "seq"), axis=0, tiled=True)
    slab_pos = lax.all_gather(key_places, ("tensor", "seq"), axis=0, tiled=True)
    total_keys = slab_pos.shape[0]
    window_keys = 512
    blocks = (
        slab_keys.reshape(total_keys // window_keys, window_keys, key_value_width),
        slab_values.reshape(total_keys // window_keys, window_keys, key_value_width),
        slab_pos.reshape(total_keys // window_keys, window_keys),
    )
    state_out, unused = lax.scan(attend_block, initial, blocks)
    attention_result = state_out[2] / state_out[1][:, :, None]
    attention_result = (
        attention_result.reshape(KEY_VALUE_HEADS, query_total, queries_per_group, HEAD_SIZE)
        .transpose(1, 0, 2, 3)
        .reshape(query_total, query_span_width)
        .astype(jnp.bfloat16)
    )
    head_block = lax.all_to_all(attention_result, "tensor", split_axis=1, concat_axis=0, tiled=True)
    result = lax.psum_scatter(
        project_rows(head_block, out_weight, kinds_group).astype(jnp.bfloat16),
        "tensor",
        scatter_dimension=0,
        tiled=True,
    )
    return result[None]


def solution(mesh):
    placed = (
        P(("groups", "seq"), "tensor", None),
        P("groups"),
        P("groups"),
        P(),
        P(None, None, "tensor"),
        P(None, "tensor"),
        P(None, "tensor", None),
    )
    return jax.shard_map(
        body,
        mesh=mesh,
        in_specs=placed,
        out_specs=P(("groups", "seq"), "tensor", None),
        check_vma=False,
    )
```

profile of v0, /device:TPU:0, one launch (start us, length us, event | category | flops | bytes accessed | tf_op | source)
XLA Modules:
  0.0 223.6 jit_solution(8450309662503764441)
XLA Ops:
  6.5 1.1 fusion.39
  7.7 0.9 slice_reduce_fusion.1
  8.6 0.8 select_reduce_fusion
  9.4 1.8 fusion.41
  11.2 0.7 gather_fusion.1
  12.0 0.7 gather_fusion.2
  14.1 13.8 %all-reduce = s32[512]{0:T(512)S(1)} all-reduce(s32[512]{0:T(512)S(1)} %fusion.47), channel_id=1, replica_groups=mesh['groups'=2,'tensor'=8,'seq'=2] {'tensor','seq'}, use_global_device_ids=true, to_apply=%add | all-reduce | flops 512 | bytes 4096
  28.9 0.7 select_reduce_fusion.1
  31.2 29.4 %all-gather.2.cloned.1.call-done = bf16[256,3584]{1,0:T(8,128)(2,1)} async-done(((bf16[32,3584]{1,0:T(8,128)(2,1)}), bf16[256,3584]{1,0:T(8,128)(2,1)}) %all-gather.2.cloned.1.call-update) | async-done | bytes 1835024 | tf_op jit(solution)/shard_map/all_gather | solution.py:69
  60.6 4.1 %fusion.19 = f32[256,576]{0,1:T(8,128)S(1)} fusion(bf16[256,3584]{1,0:T(8,128)(2,1)} %all-gather.2.cloned.1.call-done, bf16[2,3584,576]{1,2,0:T(8,128)(2,1)} %param.15), kind=kOutput, calls=%fused_computation.33 | convolution fusion | flops 1056964608 | bytes 6553600 | tf_op jit(solution)/shard_map/dot_general | solution.py:41
  64.7 1.0 copy-done.2
  65.7 2.8 %fusion.36 = bf16[256,576]{0,1:T(8,128)(2,1)S(1)} fusion(f32[256,576]{0,1:T(8,128)S(1)} %fusion.19, bf16[256,3584]{1,0:T(8,128)(2,1)} %all-gather.2.cloned.1.call-done, bf16[2,3584,576]{1,2,0:T(8,128)(2,1)S(1)} %copy-done.2, f32[576]{0:T(1024)S(1)} %get-tuple-element.271, f32[576]{0:T(1024)S(1)} %get-tuple-element.270, ...), kind=kOutput, calls=%fused_computation.46 | convolution fusion | flops 1057554432 | bytes 6857216 | tf_op jit(solution)/shard_map/dot_general | solution.py:42
  68.5 0.9 copy.50
  69.4 3.6 %all-to-all-start = ((bf16[8,32,576]{2,1,0:T(8,128)(2,1)}), bf16[8,32,576]{2,1,0:T(8,128)(2,1)S(1)}, u32[]{:S(2)}, u32[]{:S(2)}) async-start(bf16[8,32,576]{2,1,0:T(8,128)(2,1)} %bitcast.7), calls=%async_computation | async-start | bytes 655360 | tf_op jit(solution)/shard_map/all_to_all | solution.py:76
  73.3 10.0 %all-to-all-done = bf16[8,32,576]{2,1,0:T(8,128)(2,1)S(1)} async-done(((bf16[8,32,576]{2,1,0:T(8,128)(2,1)}), bf16[8,32,576]{2,1,0:T(8,128)(2,1)S(1)}, u32[]{:S(2)}, u32[]{:S(2)}) %all-to-all-start) | async-done | bytes 294944 | tf_op jit(solution)/shard_map/all_to_all | solution.py:76
  84.1 20.8 %all_gather.14 = bf16[512,512]{1,0:T(8,128)(2,1)S(1)} all-gather(bf16[32,512]{1,0:T(8,128)(2,1)S(1)} %fusion.43), channel_id=1, replica_groups=mesh['groups'=2,'tensor'=8,'seq'=2] {'tensor','seq'}, dimensions={0}, use_global_device_ids=true | all-gather | bytes 557056 | tf_op jit(solution)/shard_map/all_gather | solution.py:146
  104.9 18.9 %all_gather.15 = bf16[512,512]{1,0:T(8,128)(2,1)S(1)} all-gather(bf16[32,512]{1,0:T(8,128)(2,1)S(1)} %get-tuple-element.278), channel_id=1, replica_groups=mesh['groups'=2,'tensor'=8,'seq'=2] {'tensor','seq'}, dimensions={0}, use_global_device_ids=true | all-gather | bytes 557056 | tf_op jit(solution)/shard_map/all_gather | solution.py:147
  125.1 6.1 %conditional.1 = ((f32[4,224]{1,0:T(4,128)S(1)}, f32[4,224,128]{2,1,0:T(8,128)S(1)})) conditional(s32[]{:T(128)} %convert_element_type.68, (s32[512]{0:T(512)S(1)}, s32[]{:T(128)}, s32[32,1]{0,1:T(1,128)S(1)}, s32[512]{0:T(512)S(1)}, s32[32]{0:T(128)S(1)}, /*index=5*/pred[32]{0:T(512)(128)(4,1)S(1)}, bf16[4,32,7,128]{3,2,0,1:T(8,128)(2,1)S(1)}, ...), branch_computations={%region_5.9_spmd, %region_8.10_spmd} | conditional | flops 241148576 | bytes 8950332 | solution.py:137
  125.2 3.5 %gather_fusion = s32[512]{0:T(512)S(1)} fusion(s32[512]{0:T(512)S(1)} %get-tuple-element.202, s32[1024]{0:T(1024)S(1)} %pad_clamp_fusion), kind=kCustom, calls=%fused_computation.1 | custom fusion | bytes 6144 | tf_op jit(solution)/shard_map/while/body/eval_jaxpr/jit(_take)/gather | solution.py:102
  130.4 0.9 convolution_add_fusion
  132.0 12.2 %all_to_all.35 = bf16[32,8,448]{2,0,1:T(8,128)(2,1)S(1)} all-to-all(bf16[32,8,448]{2,0,1:T(8,128)(2,1)S(1)} %copy.55), channel_id=1, replica_groups=mesh['groups'=2,'tensor'=8,'seq'=2] {'tensor'}, dimensions={1} | all-to-all | bytes 458752 | tf_op jit(solution)/shard_map/all_to_all | solution.py:164
  144.2 3.0 %fusion.26 = bf16[256,3584]{1,0:T(8,128)(2,1)S(1)} fusion(bf16[256,448]{1,0:T(8,128)(2,1)S(1)} %bitcast.83, bf16[2,448,3584]{2,1,0:T(8,128)(2,1)} %param.17), kind=kOutput, calls=%fused_computation.40 | convolution fusion | flops 822083584 | bytes 5275648 | tf_op jit(solution)/shard_map/dot_general | solution.py:42
  147.2 4.3 %fusion.18 = bf16[256,3584]{1,0:T(8,128)(2,1)} fusion(bf16[256,3584]{1,0:T(8,128)(2,1)S(1)} %fusion.26, bf16[256,448]{1,0:T(8,128)(2,1)S(1)} %bitcast.84, bf16[2,448,3584]{2,1,0:T(8,128)(2,1)} %param.17, pred[256]{0:T(512)(128)(4,1)S(1)} %dynamic-slice_compare_fusion), kind=kOutput, calls=%fused_computation.32 | convolution fusion | flops 823001088 | bytes 7110912 | tf_op jit(solution)/shard_map/dot_general | solution.py:41
  151.6 65.2 %reduce-scatter.2.cloned.1.call-done = bf16[32,3584]{1,0:T(8,128)(2,1)} async-done(((bf16[256,3584]{1,0:T(8,128)(2,1)}), bf16[32,3584]{1,0:T(8,128)(2,1)}) %reduce-scatter.2.cloned.1.call-update) | async-done | bytes 229392 | tf_op jit(solution)/shard_map/reduce_scatter | solution.py:165
  (63 shorter events, 6.6 us)
Async XLA Ops:
  6.5 6.1 %copy-start.3 = (u32[32]{0:T(128)S(1)}, u32[32]{0:T(128)}, u32[]{:S(2)}) copy-start(u32[32]{0:T(128)} %constant.116) | copy-start | bytes 388
  6.5 5.4 %copy-start = (s32[512]{0:T(512)S(1)}, s32[512]{0:T(512)}, u32[]{:S(2)}) copy-start(s32[512]{0:T(512)} %param.12) | copy-start | bytes 6148
  6.5 24.4 %copy-start.1 = (bf16[2,576]{1,0:T(2,128)(2,1)S(1)}, bf16[2,576]{1,0:T(2,128)(2,1)}, u32[]{:S(2)}) copy-start(bf16[2,576]{1,0:T(2,128)(2,1)} %param.16) | copy-start | bytes 6916
  6.5 54.0 %all-gather.2.cloned.1.call-start = ((), (), s32[]{:S(2)}) async-start(), calls=%async_computation.3 | async-start | bytes 2064384 | tf_op jit(solution)/shard_map/all_gather | solution.py:69
  60.6 5.1 %copy-start.2 = (bf16[2,3584,576]{1,2,0:T(8,128)(2,1)S(1)}, bf16[2,3584,576]{1,2,0:T(8,128)(2,1)}, u32[]{:S(2)}) copy-start(bf16[2,3584,576]{1,2,0:T(8,128)(2,1)} %param.15) | copy-start | bytes 24772612
  69.4 13.9 %all-to-all-start = ((bf16[8,32,576]{2,1,0:T(8,128)(2,1)}), bf16[8,32,576]{2,1,0:T(8,128)(2,1)S(1)}, u32[]{:S(2)}, u32[]{:S(2)}) async-start(bf16[8,32,576]{2,1,0:T(8,128)(2,1)} %bitcast.7), calls=%async_computation | async-start | bytes 655360 | tf_op jit(solution)/shard_map/all_to_all | solution.py:76
  73.0 143.8 %reduce-scatter.2.cloned.1.call-start = ((), (), s32[]{:S(2)}) async-start(), calls=%async_computation.4 | async-start | bytes 2064384 | tf_op jit(solution)/shard_map/reduce_scatter | solution.py:165
Sparse Core Ops, SparseCore 0:
  11.3 49.2 all-gather.1
  151.7 65.0 reduce-scatter.1
where the time goes:
time: 224 us
  waiting for transfers between devices  105 us (47%)
  blocking collectives  65.7 us (29%)
  between operations  15.8 us (7%)
  matrix products  15.7 us (7%)
  local copies, waits for them, and re-layouts  9.94 us (4%)
  other arithmetic  8.05 us (4%)
  starting transfers between devices  3.67 us (2%)
    reduce_scatter x1, waiting for transfers between devices, body(): lax.psum_scatter(project_rows(head_block, out_weight, kinds_group).astype...  65.2 us
    all_gather x1, waiting for transfers between devices, body(): lax.all_gather(normed, 'tensor', axis=0, tiled=True)  29.4 us
    all_gather x1, blocking collectives, body(): lax.all_gather(key_row_values, ('tensor', 'seq'), axis=0, tiled=True)  20.8 us
    all_gather x1, blocking collectives, body(): lax.all_gather(value_matrix, ('tensor', 'seq'), axis=0, tiled=True)  18.9 us
    unnamed x1, blocking collectives  13.8 us
    all_to_all x1, blocking collectives, body(): lax.all_to_all(attention_result, 'tensor', split_axis=1, concat_axis=0, t...  12.2 us
    all_to_all x1, waiting for transfers between devices, body(): lax.all_to_all(column_block, 'tensor', split_axis=0, concat_axis=1, tiled...  10 us
    dot_general x2, matrix products, both_kinds(): jnp.dot(row_slab, weights[0], preferred_element_type=jnp.float32)  8.46 us
  transfers between devices with their start and end apart: 3, of which 3 were waited for; matrix products, arithmetic and copies ran while one was open for 2% of the time, Pallas kernels for 0%

commit v1 on v0

--- a/solution.py
+++ b/solution.py
@@ -81,85 +81,53 @@
         KEY_VALUE_HEADS,
     )
     value_matrix = row_tile[:, query_span_width + key_value_width :]
-    query_sections = jnp.take(section_of_row, key_places)
-    query_image = jnp.take(kinds_all, key_places) == 1
-    section_last = (
-        jnp.sum((section_of_row[None, :] <= query_sections[:, None]).astype(jnp.int32), axis=1) - 1
+    slab = lax.all_gather(
+        jnp.concatenate([key_row_values, value_matrix], axis=1), ("tensor", "seq"), axis=0, tiled=True
     )
-    reach_rows = jnp.where(query_image, section_last, key_places)
-    reach_most = jnp.max(reach_rows)
-    query_total = query_matrix.shape[0]
-    grouped_queries = (
-        query_matrix.reshape(query_total, KEY_VALUE_HEADS, queries_per_group, HEAD_SIZE)
-        .transpose(1, 0, 2, 3)
-        .reshape(KEY_VALUE_HEADS, query_total * queries_per_group, HEAD_SIZE)
+    seq_size = lax.axis_size("seq")
+    total_keys = own_rows * tensor_size * seq_size
+    sections_grid = section_of_row.reshape(seq_size, tensor_size, own_rows)
+    key_sections = sections_grid.transpose(1, 0, 2).reshape(total_keys)
+    key_pos = (
+        jnp.arange(total_keys, dtype=jnp.int32)
+        .reshape(seq_size, tensor_size, own_rows)
+        .transpose(1, 0, 2)
+        .reshape(total_keys)
     )
-    scale_factor = 1.0 / math.sqrt(HEAD_SIZE)
-
-    def attend_block(state_in, key_block):
-        key_tile, value_tile, key_pos = key_block
-        window_keys = key_pos.shape[0]
-        key_sections = jnp.take(section_of_row, key_pos)
-        allowed = (key_pos[None, :] <= key_places[:, None]) | (
-            key_sections[None, :] == query_sections[:, None]
-        ) & query_image[:, None]
-        allowed = jnp.broadcast_to(
-            allowed[:, None, :], (query_total, queries_per_group, window_keys)
-        ).reshape(1, query_total * queries_per_group, window_keys)
-        key_head_tensor = key_tile.reshape(window_keys, KEY_VALUE_HEADS, HEAD_SIZE)
-        value_head_tensor = value_tile.reshape(window_keys, KEY_VALUE_HEADS, HEAD_SIZE)
-
-        def update(state_now):
-            running_max, running_sum, running_acc = state_now
-            scores = (
-                jnp.einsum(
-                    "gqa,kga->gqk",
-                    grouped_queries,
-                    key_head_tensor,
-                    preferred_element_type=jnp.float32,
-                )
-                * scale_factor
-            )
-            scores = jnp.where(allowed, scores, BLOCKED_SCORE)
-            new_max = jnp.maximum(running_max, jnp.max(scores, axis=2))
-            shrink = jnp.exp(running_max - new_max)
-            weights = jnp.where(allowed, jnp.exp(scores - new_max[:, :, None]), 0.0)
-            new_sum = running_sum * shrink + jnp.sum(weights, axis=2)
-            new_acc = running_acc * shrink[:, :, None] + jnp.einsum(
-                "gqk,kga->gqa",
-                weights.astype(jnp.bfloat16),
-                value_head_tensor,
-                preferred_element_type=jnp.float32,
-            )
-            return (new_max, new_sum, new_acc)
-
-        return (
-            lax.cond(jnp.min(key_pos) > reach_most, lambda state_now: state_now, update, state_in),
-            None,
-        )
-
-    initial = (
-        jnp.full((KEY_VALUE_HEADS, query_total * queries_per_group), BLOCKED_SCORE, jnp.float32),
-        jnp.zeros((KEY_VALUE_HEADS, query_total * queries_per_group), jnp.float32),
-        jnp.zeros((KEY_VALUE_HEADS, query_total * queries_per_group, HEAD_SIZE), jnp.float32),
+    query_sections = lax.dynamic_slice_in_dim(
+        section_of_row, group_start + tensor_rank * own_rows, own_rows
     )
-    slab_keys = lax.all_gather(key_row_values, ("tensor", "seq"), axis=0, tiled=True)
-    slab_values = lax.all_gather(value_matrix, ("tensor", "seq"), axis=0, tiled=True)
-    slab_pos = lax.all_gather(key_places, ("tensor", "seq"), axis=0, tiled=True)
-    total_keys = slab_pos.shape[0]
-    window_keys = 512
-    blocks = (
-        slab_keys.reshape(total_keys // window_keys, window_keys, key_value_width),
-        slab_values.reshape(total_keys // window_keys, window_keys, key_value_width),
-        slab_pos.reshape(total_keys // window_keys, window_keys),
+    query_image = own_kinds == 1
+    allowed = (key_pos[None, :] <= key_places[:, None]) | (
+        key_sections[None, :] == query_sections[:, None]
+    ) & query_image[:, None]
+    grouped_queries = query_matrix.reshape(own_rows, KEY_VALUE_HEADS, queries_per_group, HEAD_SIZE)
+    grouped_queries = grouped_queries.transpose(1, 2, 0, 3).reshape(
+        KEY_VALUE_HEADS, queries_per_group * own_rows, HEAD_SIZE
     )
-    state_out, unused = lax.scan(attend_block, initial, blocks)
-    attention_result = state_out[2] / state_out[1][:, :, None]
+    key_heads = slab[:, :key_value_width].reshape(total_keys, KEY_VALUE_HEADS, HEAD_SIZE)
+    value_heads = slab[:, key_value_width:].reshape(total_keys, KEY_VALUE_HEADS, HEAD_SIZE)
+    scores = jnp.einsum(
+        "gqa,kga->gqk", grouped_queries, key_heads, preferred_element_type=jnp.float32
+    ) * (1.0 / math.sqrt(HEAD_SIZE))
+    allowed = jnp.broadcast_to(
+        allowed[None, None], (1, queries_per_group, own_rows, total_keys)
+    ).reshape(1, queries_per_group * own_rows, total_keys)
+    scores = jnp.where(allowed, scores, BLOCKED_SCORE)
+    peak = jnp.max(scores, axis=2, keepdims=True)
+    weights = jnp.where(allowed, jnp.exp(scores - peak), 0.0)
+    total = jnp.sum(weights, axis=2)
+    summed = jnp.einsum(
+        "gqk,kga->gqa",
+        weights.astype(jnp.bfloat16),
+        value_heads,
+        preferred_element_type=jnp.float32,
+    )
+    attention_result = (summed / total[:, :, None]).astype(jnp.bfloat16)
     attention_result = (
-        attention_result.reshape(KEY_VALUE_HEADS, query_total, queries_per_group, HEAD_SIZE)
-        .transpose(1, 0, 2, 3)
-        .reshape(query_total, query_span_width)
-        .astype(jnp.bfloat16)
+        attention_result.reshape(KEY_VALUE_HEADS, queries_per_group, own_rows, HEAD_SIZE)
+        .transpose(2, 0, 1, 3)
+        .reshape(own_rows, query_span_width)
     )
     head_block = lax.all_to_all(attention_result, "tensor", split_axis=1, concat_axis=0, tiled=True)
     result = lax.psum_scatter(

time: 224 us -> 218 us (0.973)
  blocking collectives: 65.7 us -> 12.7 us
  waiting for transfers between devices: 105 us -> 158 us
  between operations: 15.8 us -> 13.3 us
  local copies, waits for them, and re-layouts: 9.94 us -> 7.5 us
    all_gather x2 -> x0, blocking collectives: 39.7 us -> none  [the longest x1 20.8 us: body(): lax.all_gather(key_row_values, ('tensor', 'seq'), axis=0, tiled=True)]
    all_gather x0 -> x1, waiting for transfers between devices: none -> 35.4 us  [body(): lax.all_gather(jnp.concatenate([key_row_values, value_matrix], axis=1), (...]
    all_gather x1, waiting for transfers between devices: 29.4 us -> 46.6 us  [body(): lax.all_gather(normed, 'tensor', axis=0, tiled=True)]
    unnamed x1 -> x0, blocking collectives: 13.8 us -> none
    gather x3 -> x0, local copies, waits for them, and re-layouts: 4.91 us -> none  [the longest x1 3.49 us: attend_block(): key_sections = jnp.take(section_of_row, key_pos)]
  transfers between devices with their start and end apart: 3 -> 4, of which waited for: 3 -> 4; matrix products, arithmetic and copies ran while one was open for 2% -> 2% of each run, Pallas kernels for 0% -> 0%
where the time goes in v1:
time: 218 us
  waiting for transfers between devices  158 us (72%)
  matrix products  16.3 us (7%)
  between operations  13.3 us (6%)
  blocking collectives  12.7 us (6%)
  local copies, waits for them, and re-layouts  7.5 us (3%)
  other arithmetic  6.68 us (3%)
  starting transfers between devices  3.73 us (2%)
    reduce_scatter x1, waiting for transfers between devices, body(): lax.psum_scatter(project_rows(head_block, out_weight, kinds_group).astype...  65.7 us
    all_gather x1, waiting for transfers between devices, body(): lax.all_gather(normed, 'tensor', axis=0, tiled=True)  46.6 us
    all_gather x1, waiting for transfers between devices, body(): lax.all_gather(jnp.concatenate([key_row_values, value_matrix], axis=1), (...  35.4 us
    all_to_all x1, blocking collectives, body(): lax.all_to_all(attention_result, 'tensor', split_axis=1, concat_axis=0, t...  12.7 us
    all_to_all x1, waiting for transfers between devices, body(): lax.all_to_all(column_block, 'tensor', split_axis=0, concat_axis=1, tiled...  9.94 us
    dot_general x2, matrix products, both_kinds(): jnp.dot(row_slab, weights[0], preferred_element_type=jnp.float32)  8.42 us
    dot_general x2, matrix products, both_kinds(): jnp.dot(row_slab, weights[1], preferred_element_type=jnp.float32)  5.78 us
  transfers between devices with their start and end apart: 4, of which 4 were waited for; matrix products, arithmetic and copies ran while one was open for 2% of the time, Pallas kernels for 0%

profile of v1, /device:TPU:0, one launch (start us, length us, event | category | flops | bytes accessed | tf_op | source)
XLA Modules:
  0.0 217.9 jit_solution(9667096528757379834)
XLA Ops:
  6.5 1.1 fusion.28
  7.6 0.9 slice_reduce_fusion.1
  8.5 0.8 select_reduce_fusion
  9.4 1.8 fusion.30
  11.2 0.8 reshape.249
  11.9 0.7 convert_element_type.51
  12.8 0.8 dynamic_slice.12
  13.7 46.6 %all-gather.3.cloned.1.call-done = bf16[256,3584]{1,0:T(8,128)(2,1)} async-done(((bf16[32,3584]{1,0:T(8,128)(2,1)}), bf16[256,3584]{1,0:T(8,128)(2,1)}) %all-gather.3.cloned.1.call-update) | async-done | bytes 1835024 | tf_op jit(solution)/shard_map/all_gather | solution.py:69
  60.3 4.1 %fusion.2 = f32[256,576]{0,1:T(8,128)S(1)} fusion(bf16[256,3584]{1,0:T(8,128)(2,1)} %all-gather.3.cloned.1.call-done, bf16[2,3584,576]{1,2,0:T(8,128)(2,1)} %param.11), kind=kOutput, calls=%fused_computation.3 | convolution fusion | flops 1056964608 | bytes 6553600 | tf_op jit(solution)/shard_map/dot_general | solution.py:41
  64.4 0.9 copy-done
  65.4 2.8 %fusion.21 = bf16[256,576]{0,1:T(8,128)(2,1)S(1)} fusion(f32[256,576]{0,1:T(8,128)S(1)} %fusion.2, bf16[256,3584]{1,0:T(8,128)(2,1)} %all-gather.3.cloned.1.call-done, bf16[2,3584,576]{1,2,0:T(8,128)(2,1)S(1)} %copy-done, f32[576]{0:T(1024)S(1)} %get-tuple-element.8, f32[576]{0:T(1024)S(1)} %get-tuple-element.7, pred[256]{0:T(512)(128)(4,1)S(1)} %dynamic-slice_compare_fusion), kind=kOutput, calls=%fused_computation.21 | convolution fusion | flops 1057554432 | bytes 6857216 | tf_op jit(solution)/shard_map/dot_general | solution.py:42
  68.1 0.9 copy.37
  69.0 3.6 %all-to-all-start = ((bf16[8,32,576]{2,1,0:T(8,128)(2,1)}), bf16[8,32,576]{2,1,0:T(8,128)(2,1)S(1)}, u32[]{:S(2)}, u32[]{:S(2)}) async-start(bf16[8,32,576]{2,1,0:T(8,128)(2,1)} %bitcast.6), calls=%async_computation | async-start | bytes 655360 | tf_op jit(solution)/shard_map/all_to_all | solution.py:76
  73.0 9.9 %all-to-all-done = bf16[8,32,576]{2,1,0:T(8,128)(2,1)S(1)} async-done(((bf16[8,32,576]{2,1,0:T(8,128)(2,1)}), bf16[8,32,576]{2,1,0:T(8,128)(2,1)S(1)}, u32[]{:S(2)}, u32[]{:S(2)}) %all-to-all-start) | async-done | bytes 294944 | tf_op jit(solution)/shard_map/all_to_all | solution.py:76
  83.6 0.6 pad_maximum_fusion
  85.0 0.6 fusion.31
  85.9 35.4 %all-gather.5.cloned.1.call-done = bf16[512,1024]{1,0:T(8,128)(2,1)} async-done(((bf16[32,1024]{1,0:T(8,128)(2,1)}), bf16[512,1024]{1,0:T(8,128)(2,1)}) %all-gather.5.cloned.1.call-update) | async-done | bytes 1048592 | tf_op jit(solution)/shard_map/all_gather | solution.py:84
  121.4 1.3 fusion.46
  123.5 0.9 fusion.47
  124.4 0.8 fusion.14
  125.7 12.7 %all_to_all.38 = bf16[32,8,448]{2,0,1:T(8,128)(2,1)S(1)} all-to-all(bf16[32,8,448]{2,0,1:T(8,128)(2,1)S(1)} %copy.45), channel_id=1, replica_groups=mesh['groups'=2,'tensor'=8,'seq'=2] {'tensor'}, dimensions={1} | all-to-all | bytes 458752 | tf_op jit(solution)/shard_map/all_to_all | solution.py:132
  138.3 3.0 %fusion.9 = bf16[256,3584]{1,0:T(8,128)(2,1)S(1)} fusion(bf16[256,448]{1,0:T(8,128)(2,1)S(1)} %bitcast.79, bf16[2,448,3584]{2,1,0:T(8,128)(2,1)} %param.13), kind=kOutput, calls=%fused_computation.10 | convolution fusion | flops 822083584 | bytes 5275648 | tf_op jit(solution)/shard_map/dot_general | solution.py:42
  141.4 4.3 %fusion.1 = bf16[256,3584]{1,0:T(8,128)(2,1)} fusion(bf16[256,3584]{1,0:T(8,128)(2,1)S(1)} %fusion.9, bf16[256,448]{1,0:T(8,128)(2,1)S(1)} %bitcast.80, bf16[2,448,3584]{2,1,0:T(8,128)(2,1)} %param.13, pred[256]{0:T(512)(128)(4,1)S(1)} %dynamic-slice_compare_fusion), kind=kOutput, calls=%fused_computation.2 | convolution fusion | flops 823001088 | bytes 7110912 | tf_op jit(solution)/shard_map/dot_general | solution.py:41
  145.7 65.7 %reduce-scatter.2.cloned.1.call-done = bf16[32,3584]{1,0:T(8,128)(2,1)} async-done(((bf16[256,3584]{1,0:T(8,128)(2,1)}), bf16[32,3584]{1,0:T(8,128)(2,1)}) %reduce-scatter.2.cloned.1.call-update) | async-done | bytes 229392 | tf_op jit(solution)/shard_map/reduce_scatter | solution.py:133
  (42 shorter events, 3.7 us)
Async XLA Ops:
  6.5 53.7 %all-gather.3.cloned.1.call-start = ((), (), s32[]{:S(2)}) async-start(), calls=%async_computation.3 | async-start | bytes 2064384 | tf_op jit(solution)/shard_map/all_gather | solution.py:69
  60.3 5.1 %copy-start = (bf16[2,3584,576]{1,2,0:T(8,128)(2,1)S(1)}, bf16[2,3584,576]{1,2,0:T(8,128)(2,1)}, u32[]{:S(2)}) copy-start(bf16[2,3584,576]{1,2,0:T(8,128)(2,1)} %param.11) | copy-start | bytes 24772612
  69.0 13.9 %all-to-all-start = ((bf16[8,32,576]{2,1,0:T(8,128)(2,1)}), bf16[8,32,576]{2,1,0:T(8,128)(2,1)S(1)}, u32[]{:S(2)}, u32[]{:S(2)}) async-start(bf16[8,32,576]{2,1,0:T(8,128)(2,1)} %bitcast.6), calls=%async_computation | async-start | bytes 655360 | tf_op jit(solution)/shard_map/all_to_all | solution.py:76
  72.7 48.7 %all-gather.5.cloned.1.call-start = ((), (), s32[]{:S(2)}) async-start(), calls=%async_computation.4 | async-start | bytes 1114112 | tf_op jit(solution)/shard_map/all_gather | solution.py:84
  84.3 127.0 %reduce-scatter.2.cloned.1.call-start = ((), (), s32[]{:S(2)}) async-start(), calls=%async_computation.5 | async-start | bytes 2064384 | tf_op jit(solution)/shard_map/reduce_scatter | solution.py:133
Sparse Core Ops, SparseCore 0:
  11.3 48.9 all-gather.2
  84.4 36.9 all-gather.4
  145.8 65.5 reduce-scatter.1

commit v2 on v1

--- a/solution.py
+++ b/solution.py
@@ -1,8 +1,11 @@
+import functools
 import math
 
 import jax
 import jax.numpy as jnp
 from jax import lax
+from jax.experimental import pallas as pl
+from jax.experimental.pallas import tpu as pltpu
 from jax.sharding import PartitionSpec as P
 
 QUERY_HEADS = 28
@@ -13,6 +16,166 @@
 NORM_EPSILON = 1e-06
 ROPE_THETA = 1000000.0
 BLOCKED_SCORE = -1e30
+
+
+MESH_ID = pl.DeviceIdType.MESH
+
+
+def greet(peers):
+    barrier = pltpu.get_barrier_semaphore()
+    for peer in peers:
+        pl.semaphore_signal(barrier, inc=1, device_id=peer, device_id_type=MESH_ID)
+    pl.semaphore_wait(barrier, len(peers))
+
+
+def gather_kernel(n, across, x_ref, out_ref, line_send, line_recv, pair_send, pair_recv, seq_send, seq_recv):
+    rank = lax.axis_index("tensor")
+    half = n // 2
+    high, low = rank // 2, rank % 2
+    slab = lax.axis_index("seq") if across else 0
+    pair = {"tensor": high * 2 + 1 - low}
+    line = [{"tensor": ((high + d) % half) * 2 + low} for d in range(1, half)]
+    other = {"seq": 1 - lax.axis_index("seq")}
+    greet(line + [pair] + ([other] if across else []))
+
+    def push(src, block, send, recv, to):
+        copy = pltpu.make_async_remote_copy(
+            src_ref=src,
+            dst_ref=out_ref.at[slab, block],
+            send_sem=send,
+            recv_sem=recv,
+            device_id=to,
+            device_id_type=MESH_ID,
+        )
+        copy.start()
+        return copy
+
+    lines = [push(x_ref, rank, line_send.at[d], line_recv.at[d], line[d]) for d in range(half - 1)]
+    pairs = [push(x_ref, rank, pair_send.at[half - 1], pair_recv.at[half - 1], pair)]
+    crossed = []
+    if across:
+        crossed.append(push(x_ref, rank, seq_send.at[n - 1], seq_recv.at[n - 1], other))
+    out_ref[slab, rank] = x_ref[...]
+    for d in range(half - 1):
+        lines[d].wait_recv()
+        block = ((high + half - d - 1) % half) * 2 + low
+        pairs.append(push(out_ref.at[slab, block], block, pair_send.at[d], pair_recv.at[d], pair))
+        if across:
+            crossed.append(
+                push(out_ref.at[slab, block], block, seq_send.at[d], seq_recv.at[d], other)
+            )
+    for d in range(half):
+        pairs[d].wait_recv()
+        if across:
+            block = ((high + half - d) % half) * 2 + 1 - low
+            at = half - 1 + d
+            crossed.append(
+                push(out_ref.at[slab, block], block, seq_send.at[at], seq_recv.at[at], other)
+            )
+    for copy in crossed:
+        copy.wait_recv()
+    for copy in lines + pairs + crossed:
+        copy.wait_send()
+
+
+def gather_rows(block, n, across, name_id):
+    rows, columns = block.shape
+    slabs = 2 if across else 1
+    return pl.pallas_call(
+        functools.partial(gather_kernel, n, across),
+        out_shape=jax.ShapeDtypeStruct((slabs, n, rows, columns), block.dtype),
+        in_specs=[pl.BlockSpec(memory_space=pltpu.VMEM)],
+        out_specs=pl.BlockSpec(memory_space=pltpu.VMEM),
+        scratch_shapes=[
+            pltpu.SemaphoreType.DMA((n // 2,)),
+            pltpu.SemaphoreType.DMA((n // 2,)),
+            pltpu.SemaphoreType.DMA((n // 2,)),
+            pltpu.SemaphoreType.DMA((n // 2,)),
+            pltpu.SemaphoreType.DMA((n,)),
+            pltpu.SemaphoreType.DMA((n,)),
+        ],
+        compiler_params=pltpu.CompilerParams(collective_id=name_id, has_side_effects=True),
+    )(block).reshape(slabs * n * rows, columns)
+
+
+def scatter_kernel(
+    n, p_ref, out_ref, stage, from_pair, from_line, pair_send, pair_recv, line_send, line_recv
+):
+    rank = lax.axis_index("tensor")
+    half = n // 2
+    high, low = rank // 2, rank % 2
+    pair = {"tensor": high * 2 + 1 - low}
+    line = [{"tensor": ((high + d) % half) * 2 + low} for d in range(1, half)]
+    greet(line + [pair])
+    order = list(range(1, half)) + [0]
+    pairs = {}
+    for d in order:
+        pairs[d] = pltpu.make_async_remote_copy(
+            src_ref=p_ref.at[((high + d) % half) * 2 + 1 - low],
+            dst_ref=from_pair.at[d],
+            send_sem=pair_send.at[d],
+            recv_sem=pair_recv.at[d],
+            device_id=pair,
+            device_id_type=MESH_ID,
+        )
+        pairs[d].start()
+    columns = p_ref.shape[2]
+    lines = []
+    for d in order:
+        pairs[d].wait_recv()
+        mine = ((high + d) % half) * 2 + low
+        if d:
+            for c in range(0, columns, 512):
+                both = p_ref[mine, :, c : c + 512].astype(jnp.float32) + from_pair[
+                    d, :, c : c + 512
+                ].astype(jnp.float32)
+                stage[d - 1, :, c : c + 512] = both.astype(jnp.bfloat16)
+            copy = pltpu.make_async_remote_copy(
+                src_ref=stage.at[d - 1],
+                dst_ref=from_line.at[d - 1],
+                send_sem=line_send.at[d - 1],
+                recv_sem=line_recv.at[d - 1],
+                device_id=line[d - 1],
+                device_id_type=MESH_ID,
+            )
+            copy.start()
+            lines.append(copy)
+    for copy in lines:
+        copy.wait_recv()
+    for c in range(0, columns, 512):
+        both = p_ref[rank, :, c : c + 512].astype(jnp.float32) + from_pair[
+            0, :, c : c + 512
+        ].astype(jnp.float32)
+        for d in range(half - 1):
+            both = both + from_line[d, :, c : c + 512].astype(jnp.float32)
+        out_ref[:, c : c + 512] = both.astype(jnp.bfloat16)
+    for d in order:
+        pairs[d].wait_send()
+    for copy in lines:
+        copy.wait_send()
+
+
+def scatter_sums(partial, n):
+    rows, columns = partial.shape[0] // n, partial.shape[1]
+    half = n // 2
+    return pl.pallas_call(
+        functools.partial(scatter_kernel, n),
+        out_shape=jax.ShapeDtypeStruct((rows, columns), partial.dtype),
+        in_specs=[pl.BlockSpec(memory_space=pltpu.VMEM)],
+        out_specs=pl.BlockSpec(memory_space=pltpu.VMEM),
+        scratch_shapes=[
+            pltpu.VMEM((half - 1, rows, columns), jnp.bfloat16),
+            pltpu.VMEM((half, rows, columns), jnp.bfloat16),
+            pltpu.VMEM((half - 1, rows, columns), jnp.bfloat16),
+            pltpu.SemaphoreType.DMA((half,)),
+            pltpu.SemaphoreType.DMA((half,)),
+            pltpu.SemaphoreType.DMA((half,)),
+            pltpu.SemaphoreType.DMA((half,)),
+        ],
+        compiler_params=pltpu.CompilerParams(
+            collective_id=2, has_side_effects=True, vmem_limit_bytes=32 * 1024 * 1024
+        ),
+    )(partial.reshape(n, rows, columns))
 
 
 def row_kinds(section_of_row, section_kind):
@@ -66,7 +229,7 @@
     normed = (features * scaled * gain_rows).astype(jnp.bfloat16)
     bias_pair = qkv_bias.astype(jnp.float32)
     product = project_rows(
-        lax.all_gather(normed, "tensor", axis=0, tiled=True), qkv_weight, kinds_group
+        gather_rows(normed, tensor_size, False, 0), qkv_weight, kinds_group
     )
     column_block = (
         product + jnp.where(kinds_group[:, None] == 1, bias_pair[1], bias_pair[0])
@@ -81,19 +244,12 @@
         KEY_VALUE_HEADS,
     )
     value_matrix = row_tile[:, query_span_width + key_value_width :]
-    slab = lax.all_gather(
-        jnp.concatenate([key_row_values, value_matrix], axis=1), ("tensor", "seq"), axis=0, tiled=True
-    )
-    seq_size = lax.axis_size("seq")
-    total_keys = own_rows * tensor_size * seq_size
-    sections_grid = section_of_row.reshape(seq_size, tensor_size, own_rows)
-    key_sections = sections_grid.transpose(1, 0, 2).reshape(total_keys)
-    key_pos = (
-        jnp.arange(total_keys, dtype=jnp.int32)
-        .reshape(seq_size, tensor_size, own_rows)
-        .transpose(1, 0, 2)
-        .reshape(total_keys)
-    )
+    slab = gather_rows(
+        jnp.concatenate([key_row_values, value_matrix], axis=1), tensor_size, True, 1
+    )
+    total_keys = slab.shape[0]
+    key_sections = section_of_row
+    key_pos = jnp.arange(total_keys, dtype=jnp.int32)
     query_sections = lax.dynamic_slice_in_dim(
         section_of_row, group_start + tensor_rank * own_rows, own_rows
     )
@@ -130,11 +286,8 @@
         .reshape(own_rows, query_span_width)
     )
     head_block = lax.all_to_all(attention_result, "tensor", split_axis=1, concat_axis=0, tiled=True)
-    result = lax.psum_scatter(
-        project_rows(head_block, out_weight, kinds_group).astype(jnp.bfloat16),
-        "tensor",
-        scatter_dimension=0,
-        tiled=True,
+    result = scatter_sums(
+        project_rows(head_block, out_weight, kinds_group).astype(jnp.bfloat16), tensor_size
     )
     return result[None]
 

time: 218 us -> 134 us (0.61)
  waiting for transfers between devices: 158 us -> 8.35 us
  Pallas kernels: 0 us -> 76.3 us
  between operations: 13.3 us -> 0.32 us
  starting transfers between devices: 3.73 us -> 7.5 us
    all_gather x2 -> x0, waiting for transfers between devices: 82 us -> none  [the longest x1 46.6 us: body(): lax.all_gather(normed, 'tensor', axis=0, tiled=True)]
    pallas_call x0 -> x3, Pallas kernels: none -> 76.3 us  [the longest x2 49.7 us: gather_rows(): pl.pallas_call(functools.partial(gather_kernel, n, across), out_shape=jax...]
    reduce_scatter x1 -> x0, waiting for transfers between devices: 65.7 us -> none  [body(): lax.psum_scatter(project_rows(head_block, out_weight, kinds_group).astype...]
    all_to_all x1, starting transfers between devices: 3.65 us -> 7.5 us  [body(): lax.all_to_all(column_block, 'tensor', split_axis=0, concat_axis=1, tiled...]
  transfers between devices with their start and end apart: 4 -> 1, of which waited for: 4 -> 1; matrix products, arithmetic and copies ran while one was open for 2% -> 0% of each run, Pallas kernels for 0% -> 0%
where the time goes in v2:
time: 134 us
  Pallas kernels  76.3 us (57%)
  matrix products  15.7 us (12%)
  blocking collectives  14 us (10%)
  waiting for transfers between devices  8.35 us (6%)
  starting transfers between devices  7.5 us (6%)
  other arithmetic  6 us (4%)
  local copies, waits for them, and re-layouts  5.63 us (4%)
    pallas_call x2, Pallas kernels, gather_rows(): pl.pallas_call(functools.partial(gather_kernel, n, across), out_shape=jax...  49.7 us
    pallas_call x1, Pallas kernels, scatter_sums(): pl.pallas_call(functools.partial(scatter_kernel, n), out_shape=jax.ShapeD...  26.6 us
    all_to_all x1, blocking collectives, body(): lax.all_to_all(attention_result, 'tensor', split_axis=1, concat_axis=0, t...  14 us
    all_to_all x1, waiting for transfers between devices, body(): lax.all_to_all(column_block, 'tensor', split_axis=0, concat_axis=1, tiled...  8.35 us
    all_to_all x1, starting transfers between devices, body(): lax.all_to_all(column_block, 'tensor', split_axis=0, concat_axis=1, tiled...  7.5 us
    dot_general x2, matrix products, both_kinds(): jnp.dot(row_slab, weights[0], preferred_element_type=jnp.float32)  7.2 us
    dot_general x2, matrix products, both_kinds(): jnp.dot(row_slab, weights[1], preferred_element_type=jnp.float32)  6.46 us
  transfers between devices with their start and end apart: 1, of which 1 were waited for; matrix products, arithmetic and copies ran while one was open for 0% of the time, Pallas kernels for 0%

profile of v2, /device:TPU:0, one launch (start us, length us, event | category | flops | bytes accessed | tf_op | source)
XLA Modules:
  0.0 133.9 jit_solution(14895657534680429264)
XLA Ops:
  0.0 1.1 fusion.28
  1.1 0.8 select_reduce_fusion
  2.1 0.9 slice_reduce_fusion.1
  2.9 1.8 %fusion.30.x_ref = bf16[32,3584]{1,0:T(8,128)(2,1)} fusion(bf16[1,32,3584]{2,1,0:T(8,128)(2,1)} %param.7, f32[32]{0:T(128)S(1)} %add_rsqrt_fusion, pred[32]{0:T(512)(128)(4,1)S(1)} %dynamic-slice_compare_fusion.1, bf16[3584]{0:T(1024)(128)(2,1)S(1)} %get-tuple-element.6, bf16[3584]{0:T(1024)(128)(2,1)S(1)} %get-tuple-element.5), kind=kLoop, calls=%fused_computation.32 | loop fusion | flops 688128 | bytes 473248 | tf_op jit(solution)/shard_map/convert_element_type | solution.py:229
  4.7 35.4 %shard_map.73 = bf16[1,8,32,3584]{3,2,1,0:T(8,128)(2,1)} custom-call(bf16[32,3584]{1,0:T(8,128)(2,1)} %fusion.30.x_ref), custom_call_target="tpu_custom_call" | custom-call | tf_op jit(solution)/shard_map/pallas_call | solution.py:84
  40.2 4.1 %fusion.2 = f32[256,576]{0,1:T(8,128)S(1)} fusion(bf16[256,3584]{1,0:T(8,128)(2,1)} %bitcast.76, bf16[2,3584,576]{1,2,0:T(8,128)(2,1)} %param.11), kind=kOutput, calls=%fused_computation.3 | convolution fusion | flops 1056964608 | bytes 6553600 | tf_op jit(solution)/shard_map/dot_general | solution.py:204
  44.4 3.4 %fusion.21 = bf16[256,576]{0,1:T(8,128)(2,1)S(1)} fusion(f32[256,576]{0,1:T(8,128)S(1)} %fusion.2, bf16[256,3584]{1,0:T(8,128)(2,1)S(1)} %bitcast.77, bf16[2,3584,576]{1,2,0:T(8,128)(2,1)} %param.11, f32[576]{0:T(1024)S(1)} %get-tuple-element.8, f32[576]{0:T(1024)S(1)} %get-tuple-element.7, pred[256]{0:T(512)(128)(4,1)S(1)} %dynamic-slice_compare_fusion), kind=kOutput, calls=%fused_computation.21 | convolution fusion | flops 1057554432 | bytes 6853376 | tf_op jit(solution)/shard_map/dot_general | solution.py:205
  47.8 0.9 copy.36
  48.7 7.5 %all-to-all-start = ((bf16[8,32,576]{2,1,0:T(8,128)(2,1)}), bf16[8,32,576]{2,1,0:T(8,128)(2,1)S(1)}, u32[]{:S(2)}, u32[]{:S(2)}) async-start(bf16[8,32,576]{2,1,0:T(8,128)(2,1)} %bitcast.6), calls=%async_computation | async-start | bytes 655360 | tf_op jit(solution)/shard_map/all_to_all | solution.py:239
  56.6 8.4 %all-to-all-done = bf16[8,32,576]{2,1,0:T(8,128)(2,1)S(1)} async-done(((bf16[8,32,576]{2,1,0:T(8,128)(2,1)}), bf16[8,32,576]{2,1,0:T(8,128)(2,1)S(1)}, u32[]{:S(2)}, u32[]{:S(2)}) %all-to-all-start) | async-done | bytes 294944 | tf_op jit(solution)/shard_map/all_to_all | solution.py:239
  65.7 0.6 pad_maximum_fusion.x_ref
  66.3 14.3 %shard_map.74 = bf16[2,8,32,1024]{3,2,1,0:T(8,128)(2,1)} custom-call(bf16[32,1024]{1,0:T(8,128)(2,1)} %pad_maximum_fusion.x_ref), custom_call_target="tpu_custom_call" | custom-call | tf_op jit(solution)/shard_map/pallas_call | solution.py:84
  80.6 1.3 fusion.47
  82.7 0.5 fusion.31
  83.2 0.3 reshape.196
  83.9 0.4 fusion.49
  84.3 0.9 fusion.48
  85.2 0.7 fusion.14
  86.1 0.2 all_to_all.32
  86.4 14.0 %all_to_all.38 = bf16[32,8,448]{2,0,1:T(8,128)(2,1)S(1)} all-to-all(bf16[32,8,448]{2,0,1:T(8,128)(2,1)S(1)} %copy.44), channel_id=1, replica_groups=mesh['groups'=2,'tensor'=8,'seq'=2] {'tensor'}, dimensions={1} | all-to-all | bytes 458752 | tf_op jit(solution)/shard_map/all_to_all | solution.py:288
  100.4 3.0 %fusion.9 = bf16[256,3584]{1,0:T(8,128)(2,1)S(1)} fusion(bf16[256,448]{1,0:T(8,128)(2,1)S(1)} %bitcast.86, bf16[2,448,3584]{2,1,0:T(8,128)(2,1)} %param.13), kind=kOutput, calls=%fused_computation.10 | convolution fusion | flops 822083584 | bytes 5275648 | tf_op jit(solution)/shard_map/dot_general | solution.py:205
  103.5 3.1 %fusion.1 = bf16[256,3584]{1,0:T(8,128)(2,1)S(1)} fusion(bf16[256,3584]{1,0:T(8,128)(2,1)S(1)} %fusion.9, bf16[256,448]{1,0:T(8,128)(2,1)S(1)} %bitcast.87, bf16[2,448,3584]{2,1,0:T(8,128)(2,1)} %param.13, pred[256]{0:T(512)(128)(4,1)S(1)} %dynamic-slice_compare_fusion), kind=kOutput, calls=%fused_computation.2 | convolution fusion | flops 823001088 | bytes 7110912 | tf_op jit(solution)/shard_map/dot_general | solution.py:204
  106.6 26.6 %shard_map.75 = bf16[32,3584]{1,0:T(8,128)(2,1)S(1)} custom-call(bf16[8,32,3584]{2,1,0:T(8,128)(2,1)S(1)} %bitcast.69), custom_call_target="tpu_custom_call" | custom-call | tf_op jit(solution)/shard_map/pallas_call | solution.py:161
  133.2 0.7 copy.60
  (36 shorter events, 2.5 us)
Async XLA Ops:
  0.0 40.2 %copy-start.2 = (bf16[2,576]{1,0:T(2,128)(2,1)S(1)}, bf16[2,576]{1,0:T(2,128)(2,1)}, u32[]{:S(2)}) copy-start(bf16[2,576]{1,0:T(2,128)(2,1)} %param.12) | copy-start | bytes 6916
  40.2 4.1 %copy-start = (bf16[1,8,32,3584]{3,2,1,0:T(8,128)(2,1)S(1)}, bf16[1,8,32,3584]{3,2,1,0:T(8,128)(2,1)}, u32[]{:S(2)}) copy-start(bf16[1,8,32,3584]{3,2,1,0:T(8,128)(2,1)} %shard_map.73) | copy-start | bytes 5505028
  44.4 11.9 %copy-start.1 = (s32[512]{0:T(512)S(1)}, s32[512]{0:T(512)}, u32[]{:S(2)}) copy-start(s32[512]{0:T(512)} %param.8) | copy-start | bytes 6148
  48.7 16.3 %all-to-all-start = ((bf16[8,32,576]{2,1,0:T(8,128)(2,1)}), bf16[8,32,576]{2,1,0:T(8,128)(2,1)S(1)}, u32[]{:S(2)}, u32[]{:S(2)}) async-start(bf16[8,32,576]{2,1,0:T(8,128)(2,1)} %bitcast.6), calls=%async_computation | async-start | bytes 655360 | tf_op jit(solution)/shard_map/all_to_all | solution.py:239

commit v3 on v2

--- a/solution.py
+++ b/solution.py
@@ -19,6 +19,7 @@
 
 
 MESH_ID = pl.DeviceIdType.MESH
+PIECES = 2
 
 
 def greet(peers):
@@ -38,40 +39,44 @@
     other = {"seq": 1 - lax.axis_index("seq")}
     greet(line + [pair] + ([other] if across else []))
 
-    def push(src, block, send, recv, to):
+    rows = x_ref.shape[0] // PIECES
+
+    def push(own, block, piece, sends, recvs, at, to):
+        span = pl.ds(piece * rows, rows)
+        spot = at * PIECES + piece
         copy = pltpu.make_async_remote_copy(
-            src_ref=src,
-            dst_ref=out_ref.at[slab, block],
-            send_sem=send,
-            recv_sem=recv,
+            src_ref=x_ref.at[span] if own else out_ref.at[slab, block, span],
+            dst_ref=out_ref.at[slab, block, span],
+            send_sem=sends.at[spot],
+            recv_sem=recvs.at[spot],
             device_id=to,
             device_id_type=MESH_ID,
         )
         copy.start()
         return copy
 
-    lines = [push(x_ref, rank, line_send.at[d], line_recv.at[d], line[d]) for d in range(half - 1)]
-    pairs = [push(x_ref, rank, pair_send.at[half - 1], pair_recv.at[half - 1], pair)]
-    crossed = []
-    if across:
-        crossed.append(push(x_ref, rank, seq_send.at[n - 1], seq_recv.at[n - 1], other))
+    lines, pairs, crossed = [], [], []
+    for c in range(PIECES):
+        for d in range(half - 1):
+            lines.append(push(True, rank, c, line_send, line_recv, d, line[d]))
+        pairs.append(push(True, rank, c, pair_send, pair_recv, half - 1, pair))
+        if across:
+            crossed.append(push(True, rank, c, seq_send, seq_recv, n - 1, other))
     out_ref[slab, rank] = x_ref[...]
-    for d in range(half - 1):
-        lines[d].wait_recv()
-        block = ((high + half - d - 1) % half) * 2 + low
-        pairs.append(push(out_ref.at[slab, block], block, pair_send.at[d], pair_recv.at[d], pair))
-        if across:
-            crossed.append(
-                push(out_ref.at[slab, block], block, seq_send.at[d], seq_recv.at[d], other)
-            )
-    for d in range(half):
-        pairs[d].wait_recv()
-        if across:
-            block = ((high + half - d) % half) * 2 + 1 - low
-            at = half - 1 + d
-            crossed.append(
-                push(out_ref.at[slab, block], block, seq_send.at[at], seq_recv.at[at], other)
-            )
+    for c in range(PIECES):
+        for d in range(half - 1):
+            lines[c * (half - 1) + d].wait_recv()
+            block = ((high + half - d - 1) % half) * 2 + low
+            pairs.append(push(False, block, c, pair_send, pair_recv, d, pair))
+            if across:
+                crossed.append(push(False, block, c, seq_send, seq_recv, d, other))
+    for i in range(half):
+        for c in range(PIECES):
+            at = c if i == 0 else PIECES + c * (half - 1) + i - 1
+            pairs[at].wait_recv()
+            if across:
+                block = ((high + half - i) % half) * 2 + 1 - low
+                crossed.append(push(False, block, c, seq_send, seq_recv, half - 1 + i, other))
     for copy in crossed:
         copy.wait_recv()
     for copy in lines + pairs + crossed:
@@ -87,12 +92,12 @@
         in_specs=[pl.BlockSpec(memory_space=pltpu.VMEM)],
         out_specs=pl.BlockSpec(memory_space=pltpu.VMEM),
         scratch_shapes=[
-            pltpu.SemaphoreType.DMA((n // 2,)),
-            pltpu.SemaphoreType.DMA((n // 2,)),
-            pltpu.SemaphoreType.DMA((n // 2,)),
-            pltpu.SemaphoreType.DMA((n // 2,)),
-            pltpu.SemaphoreType.DMA((n,)),
-            pltpu.SemaphoreType.DMA((n,)),
+            pltpu.SemaphoreType.DMA((n // 2 * PIECES,)),
+            pltpu.SemaphoreType.DMA((n // 2 * PIECES,)),
+            pltpu.SemaphoreType.DMA((n // 2 * PIECES,)),
+            pltpu.SemaphoreType.DMA((n // 2 * PIECES,)),
+            pltpu.SemaphoreType.DMA((n * PIECES,)),
+            pltpu.SemaphoreType.DMA((n * PIECES,)),
         ],
         compiler_params=pltpu.CompilerParams(collective_id=name_id, has_side_effects=True),
     )(block).reshape(slabs * n * rows, columns)

time: 134 us -> 132 us (0.985)
  Pallas kernels: 76.3 us -> 74 us
    pallas_call x2, Pallas kernels: 49.7 us -> 47.4 us  [gather_rows(): pl.pallas_call(functools.partial(gather_kernel, n, across), out_shape=jax...]
where the time goes in v3:
time: 132 us; the launch traced here: 131 us
  Pallas kernels  74 us (56%)
  matrix products  15.7 us (12%)
  blocking collectives  14 us (11%)
  waiting for transfers between devices  8.57 us (6%)
  starting transfers between devices  6.74 us (5%)
  other arithmetic  6 us (5%)
  local copies, waits for them, and re-layouts  5.63 us (4%)
    pallas_call x2, Pallas kernels, gather_rows(): pl.pallas_call(functools.partial(gather_kernel, n, across), out_shape=jax...  47.4 us
    pallas_call x1, Pallas kernels, scatter_sums(): pl.pallas_call(functools.partial(scatter_kernel, n), out_shape=jax.ShapeD...  26.6 us
    all_to_all x1, blocking collectives, body(): lax.all_to_all(attention_result, 'tensor', split_axis=1, concat_axis=0, t...  14 us
    all_to_all x1, waiting for transfers between devices, body(): lax.all_to_all(column_block, 'tensor', split_axis=0, concat_axis=1, tiled...  8.57 us
    dot_general x2, matrix products, both_kinds(): jnp.dot(row_slab, weights[0], preferred_element_type=jnp.float32)  7.19 us
    all_to_all x1, starting transfers between devices, body(): lax.all_to_all(column_block, 'tensor', split_axis=0, concat_axis=1, tiled...  6.74 us
    dot_general x2, matrix products, both_kinds(): jnp.dot(row_slab, weights[1], preferred_element_type=jnp.float32)  6.47 us
  transfers between devices with their start and end apart: 1, of which 1 were waited for; matrix products, arithmetic and copies ran while one was open for 0% of the time, Pallas kernels for 0%

profile of v3, /device:TPU:0, one launch (start us, length us, event | category | flops | bytes accessed | tf_op | source)
XLA Modules:
  0.0 131.0 jit_solution(17102638407261770467)
XLA Ops:
  0.0 1.1 fusion.28
  1.1 0.8 select_reduce_fusion
  2.1 0.9 slice_reduce_fusion.1
  2.9 1.8 %fusion.30.x_ref = bf16[32,3584]{1,0:T(8,128)(2,1)} fusion(bf16[1,32,3584]{2,1,0:T(8,128)(2,1)} %param.7, f32[32]{0:T(128)S(1)} %add_rsqrt_fusion, pred[32]{0:T(512)(128)(4,1)S(1)} %dynamic-slice_compare_fusion.1, bf16[3584]{0:T(1024)(128)(2,1)S(1)} %get-tuple-element.6, bf16[3584]{0:T(1024)(128)(2,1)S(1)} %get-tuple-element.5), kind=kLoop, calls=%fused_computation.32 | loop fusion | flops 688128 | bytes 473248 | tf_op jit(solution)/shard_map/convert_element_type | solution.py:234
  4.7 33.2 %shard_map.73 = bf16[1,8,32,3584]{3,2,1,0:T(8,128)(2,1)} custom-call(bf16[32,3584]{1,0:T(8,128)(2,1)} %fusion.30.x_ref), custom_call_target="tpu_custom_call" | custom-call | tf_op jit(solution)/shard_map/pallas_call | solution.py:89
  38.0 4.1 %fusion.2 = f32[256,576]{0,1:T(8,128)S(1)} fusion(bf16[256,3584]{1,0:T(8,128)(2,1)} %bitcast.76, bf16[2,3584,576]{1,2,0:T(8,128)(2,1)} %param.11), kind=kOutput, calls=%fused_computation.3 | convolution fusion | flops 1056964608 | bytes 6553600 | tf_op jit(solution)/shard_map/dot_general | solution.py:209
  42.2 3.4 %fusion.21 = bf16[256,576]{0,1:T(8,128)(2,1)S(1)} fusion(f32[256,576]{0,1:T(8,128)S(1)} %fusion.2, bf16[256,3584]{1,0:T(8,128)(2,1)S(1)} %bitcast.77, bf16[2,3584,576]{1,2,0:T(8,128)(2,1)} %param.11, f32[576]{0:T(1024)S(1)} %get-tuple-element.8, f32[576]{0:T(1024)S(1)} %get-tuple-element.7, pred[256]{0:T(512)(128)(4,1)S(1)} %dynamic-slice_compare_fusion), kind=kOutput, calls=%fused_computation.21 | convolution fusion | flops 1057554432 | bytes 6853376 | tf_op jit(solution)/shard_map/dot_general | solution.py:210
  45.6 0.9 copy.36
  46.5 6.7 %all-to-all-start = ((bf16[8,32,576]{2,1,0:T(8,128)(2,1)}), bf16[8,32,576]{2,1,0:T(8,128)(2,1)S(1)}, u32[]{:S(2)}, u32[]{:S(2)}) async-start(bf16[8,32,576]{2,1,0:T(8,128)(2,1)} %bitcast.6), calls=%async_computation | async-start | bytes 655360 | tf_op jit(solution)/shard_map/all_to_all | solution.py:244
  53.7 8.6 %all-to-all-done = bf16[8,32,576]{2,1,0:T(8,128)(2,1)S(1)} async-done(((bf16[8,32,576]{2,1,0:T(8,128)(2,1)}), bf16[8,32,576]{2,1,0:T(8,128)(2,1)S(1)}, u32[]{:S(2)}, u32[]{:S(2)}) %all-to-all-start) | async-done | bytes 294944 | tf_op jit(solution)/shard_map/all_to_all | solution.py:244
  62.9 0.6 pad_maximum_fusion.x_ref
  63.6 14.2 %shard_map.74 = bf16[2,8,32,1024]{3,2,1,0:T(8,128)(2,1)} custom-call(bf16[32,1024]{1,0:T(8,128)(2,1)} %pad_maximum_fusion.x_ref), custom_call_target="tpu_custom_call" | custom-call | tf_op jit(solution)/shard_map/pallas_call | solution.py:89
  77.8 1.3 fusion.47
  79.8 0.5 fusion.31
  80.4 0.3 reshape.196
  81.0 0.4 fusion.49
  81.4 0.9 fusion.48
  82.4 0.7 fusion.14
  83.2 0.2 all_to_all.32
  83.6 14.0 %all_to_all.38 = bf16[32,8,448]{2,0,1:T(8,128)(2,1)S(1)} all-to-all(bf16[32,8,448]{2,0,1:T(8,128)(2,1)S(1)} %copy.44), channel_id=1, replica_groups=mesh['groups'=2,'tensor'=8,'seq'=2] {'tensor'}, dimensions={1} | all-to-all | bytes 458752 | tf_op jit(solution)/shard_map/all_to_all | solution.py:293
  97.6 3.0 %fusion.9 = bf16[256,3584]{1,0:T(8,128)(2,1)S(1)} fusion(bf16[256,448]{1,0:T(8,128)(2,1)S(1)} %bitcast.86, bf16[2,448,3584]{2,1,0:T(8,128)(2,1)} %param.13), kind=kOutput, calls=%fused_computation.10 | convolution fusion | flops 822083584 | bytes 5275648 | tf_op jit(solution)/shard_map/dot_general | solution.py:210
  100.6 3.1 %fusion.1 = bf16[256,3584]{1,0:T(8,128)(2,1)S(1)} fusion(bf16[256,3584]{1,0:T(8,128)(2,1)S(1)} %fusion.9, bf16[256,448]{1,0:T(8,128)(2,1)S(1)} %bitcast.87, bf16[2,448,3584]{2,1,0:T(8,128)(2,1)} %param.13, pred[256]{0:T(512)(128)(4,1)S(1)} %dynamic-slice_compare_fusion), kind=kOutput, calls=%fused_computation.2 | convolution fusion | flops 823001088 | bytes 7110912 | tf_op jit(solution)/shard_map/dot_general | solution.py:209
  103.7 26.6 %shard_map.75 = bf16[32,3584]{1,0:T(8,128)(2,1)S(1)} custom-call(bf16[8,32,3584]{2,1,0:T(8,128)(2,1)S(1)} %bitcast.69), custom_call_target="tpu_custom_call" | custom-call | tf_op jit(solution)/shard_map/pallas_call | solution.py:166
  130.3 0.7 copy.60
  (36 shorter events, 2.5 us)
Async XLA Ops:
  0.0 38.0 %copy-start.2 = (bf16[2,576]{1,0:T(2,128)(2,1)S(1)}, bf16[2,576]{1,0:T(2,128)(2,1)}, u32[]{:S(2)}) copy-start(bf16[2,576]{1,0:T(2,128)(2,1)} %param.12) | copy-start | bytes 6916
  38.0 4.1 %copy-start = (bf16[1,8,32,3584]{3,2,1,0:T(8,128)(2,1)S(1)}, bf16[1,8,32,3584]{3,2,1,0:T(8,128)(2,1)}, u32[]{:S(2)}) copy-start(bf16[1,8,32,3584]{3,2,1,0:T(8,128)(2,1)} %shard_map.73) | copy-start | bytes 5505028
  42.1 11.1 %copy-start.1 = (s32[512]{0:T(512)S(1)}, s32[512]{0:T(512)}, u32[]{:S(2)}) copy-start(s32[512]{0:T(512)} %param.8) | copy-start | bytes 6148
  46.5 15.7 %all-to-all-start = ((bf16[8,32,576]{2,1,0:T(8,128)(2,1)}), bf16[8,32,576]{2,1,0:T(8,128)(2,1)S(1)}, u32[]{:S(2)}, u32[]{:S(2)}) async-start(bf16[8,32,576]{2,1,0:T(8,128)(2,1)} %bitcast.6), calls=%async_computation | async-start | bytes 655360 | tf_op jit(solution)/shard_map/all_to_all | solution.py:244
